TPU v7x, 32 devices: a whole 2x2x4 slice. The times are simulated.
32 devices in a mesh: groups: 2 (over y), gx: 16 (over z, x, core).
Axes of the slice: x: 2, y: 2, z: 4, core: 2. Of those that a mesh axis runs over, the one named last changes fastest.
Arguments:
- node_feats: bfloat16 [8192, 512], P(('groups', 'gx')), parts along dimension 0, may hold values from -6 to 6
- cotangent: bfloat16 [8192, 512], P(('groups', 'gx')), parts along dimension 0, may hold values from -6 to 6
- tile_val: bfloat16 [64, 4, 128, 128], P(('groups', 'gx')), parts along dimension 0, may hold values from -0.25 to 0.25
- tile_src: int32 [64, 4], P(('groups', 'gx')), parts along dimension 0, may hold values from 0 to 3
- halo_list: int32 [32, 2, 1], P(('groups', 'gx')), parts along dimension 0, may hold values from 0 to 1, as said below
- block_count: int32 [32], P(('groups', 'gx')), parts along dimension 0, may hold values from 1 to 2, as said below
- coarse_src: int32 [64, 4], P(('groups', 'gx')), parts along dimension 0, may hold values from 0 to 3
- coarse_val: float32 [64, 4], P(('groups', 'gx')), parts along dimension 0, may hold values from -3 to 3
- w_self: bfloat16 [2, 512, 512], replicated, may hold values from -0.25 to 0.25
- w_agg: bfloat16 [2, 512, 512], replicated, may hold values from -0.25 to 0.25
- w_out: bfloat16 [2, 512, 512], replicated, may hold values from -0.25 to 0.25
- norm_gain: float32 [2, 512], replicated, may hold values from 0.5 to 1.5
Outputs:
- out_feats: bfloat16 [8192, 512], P(('groups', 'gx')), parts along dimension 0
- feats_grad: bfloat16 [8192, 512], P(('groups', 'gx')), parts along dimension 0
- self_grad: bfloat16 [4, 512, 512], P('groups'), parts along dimension 0
- agg_grad: bfloat16 [4, 512, 512], P('groups'), parts along dimension 0
- out_grad: bfloat16 [4, 512, 512], P('groups'), parts along dimension 0
- gain_grad: float32 [4, 512], P('groups'), parts along dimension 0
There are 2 independent parts, one for each index of `groups`. A program takes and returns all parts, laid end to end along the dimension named above; an argument that names none is the same for every part. Nothing has to cross between parts.
Inputs may be any that keep to these rules, and one draw needn't show every extreme that they name: block_count is reached at both ends: some partition has 2 blocks and some has 1. halo_list[p, s, j] names a block of partition p below block_count[p]; blocks may repeat.
All inputs are finite; a program needn't handle non-finite values.
Results may differ from a plain program's by a relative error of at most 0.017.
Values may be sent and summed in bfloat16 or wider, within the bound.
A program may use at most 64 MiB of HBM per device.

v0:
```python
import functools

import jax
import jax.numpy as jnp
from jax import lax
from jax.experimental import pallas as pl
from jax.experimental.pallas import tpu as pltpu
from jax.sharding import PartitionSpec as P

NORM_EPSILON = 1e-05
MESH = pl.DeviceIdType.MESH
F32 = jnp.float32
BF16 = jnp.bfloat16
ALIGN = 16


def dot(left, right, left_dim, right_dim):
    return lax.dot_general(
        left, right, (((left_dim,), (right_dim,)), ((), ())), preferred_element_type=F32
    )


def reduce_plan(rows, bits):
    plan = []
    for bit in bits:
        halves = rows % (2 * ALIGN) == 0
        if halves:
            rows //= 2
        plan.append((bit, rows, halves))
    return plan


def dim_orders(count):
    bits = []
    while 2 ** (len(bits) + 1) <= count:
        bits.append(len(bits))
    swapped = list(bits)
    if len(bits) >= 3:
        swapped[1], swapped[2] = swapped[2], swapped[1]
    return bits, swapped


class Sems:
    def __init__(self, ref):
        self.ref, self.used = ref, 0

    def take(self):
        self.used += 1
        return self.ref.at[self.used - 1]


def kernel(
    count,
    sem_count,
    tile_src,
    halo_list,
    block_count,
    coarse_src,
    coarse_val,
    feats_hbm,
    cotan_hbm,
    tiles_hbm,
    wself_hbm,
    wagg_hbm,
    wout_hbm,
    gain_vm,
    out_feats_hbm,
    feats_grad_hbm,
    self_grad_hbm,
    agg_grad_hbm,
    out_grad_hbm,
    gain_grad_vm,
    feats,
    cotan,
    tiles,
    wself,
    wagg,
    wout,
    adj,
    ext,
    halo_send,
    agg,
    pre,
    hidden,
    normed,
    inv_std,
    out_feats,
    feats_grad,
    back_send,
    back_recv,
    grads,
    red_send,
    red_recv,
    full,
    gain_send,
    gain_recv,
    sem_ref,
):
    sems = Sems(sem_ref)
    layers, width = gain_vm.shape
    nblocks, ktiles, blk, _ = tiles.shape
    rows = nblocks * blk
    slab = 3 * width

    me = lax.axis_index("gx")
    parity = me % 2
    sibling = me + 1 - 2 * parity
    across = me - 1 + 2 * parity
    other = (across + count) % count
    has_other = jnp.where(across == other, 1.0, 0.0).astype(F32)
    bits, swapped = dim_orders(count)

    def bit_of(bit):
        return (me // 2**bit) % 2

    def partner(bit):
        return me + (1 - 2 * bit_of(bit)) * 2**bit

    def local(src, dst):
        copy = pltpu.make_async_copy(src, dst, sems.take())
        copy.start()
        return copy

    def remote(src, dst, to):
        copy = pltpu.make_async_remote_copy(
            src_ref=src,
            dst_ref=dst,
            send_sem=sems.take(),
            recv_sem=sems.take(),
            device_id={"gx": to},
            device_id_type=MESH,
        )
        copy.start()
        return copy

    get_feats = local(feats_hbm, feats)
    get_tiles = local(tiles_hbm, tiles)
    get_wself = local(wself_hbm, wself)
    get_wagg = local(wagg_hbm, wagg)
    get_wout = local(wout_hbm, wout)
    get_cotan = local(cotan_hbm, cotan)

    barrier = pltpu.get_barrier_semaphore()
    peers = [partner(bit) for bit in bits] + [other]
    for peer in peers:
        pl.semaphore_signal(barrier, inc=1, device_id={"gx": peer}, device_id_type=MESH)

    row_ids = lax.broadcasted_iota(jnp.int32, (rows, 1), 0)
    mask = jnp.where(row_ids < block_count[0] * blk, 1.0, 0.0).astype(F32)
    halo_0, halo_1 = halo_list[0, 0, 0], halo_list[0, 1, 0]
    to_sibling = halo_1 + (halo_0 - halo_1) * parity
    to_other = halo_0 + (halo_1 - halo_0) * parity

    def hot(index, block):
        return jnp.where(index == block, 1.0, 0.0).astype(F32)

    def pick(ref, index):
        chosen = hot(index, 0) * ref[pl.ds(0, blk), :].astype(F32)
        for block in range(1, nblocks):
            chosen += hot(index, block) * ref[pl.ds(block * blk, blk), :].astype(F32)
        return chosen.astype(BF16)

    def start_halo(layer):
        here = ext.at[layer]
        halo_send[layer, pl.ds(0, blk), :] = pick(here, to_other)
        first = remote(
            halo_send.at[layer, pl.ds(0, blk)], ext.at[layer, pl.ds(rows, blk)], other
        )
        halo_send[layer, pl.ds(blk, blk), :] = pick(here, to_sibling)
        second = remote(
            ext.at[layer, pl.ds(0, rows)], ext.at[layer, pl.ds(rows + 2 * blk, rows)], sibling
        )
        third = remote(
            halo_send.at[layer, pl.ds(blk, blk)], ext.at[layer, pl.ds(rows + blk, blk)], sibling
        )
        return (first, second, third)

    get_feats.wait()
    ext[0, pl.ds(0, rows), :] = (feats[...].astype(F32) * mask).astype(BF16)
    pl.semaphore_wait(barrier, len(peers))
    halo = start_halo(0)

    get_tiles.wait()
    eye = (
        lax.broadcasted_iota(jnp.int32, (blk, blk), 0)
        == lax.broadcasted_iota(jnp.int32, (blk, blk), 1)
    )
    lower_at, upper_at = 0, nblocks + 1
    for d in range(nblocks):
        tile_f = [tiles[d, k].astype(F32) for k in range(ktiles)]
        srcs = [tile_src[d, k] for k in range(ktiles)]

        def tile_sum(slot, tile_f=tile_f, srcs=srcs):
            total = hot(srcs[0], slot) * tile_f[0]
            for k in range(1, ktiles):
                total += hot(srcs[k], slot) * tile_f[k]
            return total

        def link(column, d=d):
            total = hot(coarse_src[d, 0], column) * coarse_val[d, 0]
            for k in range(1, coarse_src.shape[1]):
                total += hot(coarse_src[d, k], column) * coarse_val[d, k]
            return total

        def put(value, column, d=d):
            adj[pl.ds(d * blk, blk), pl.ds(column * blk, blk)] = value.astype(BF16)

        for j in range(nblocks):
            own = link(nblocks * parity + j)
            put(tile_sum(1 + j) + jnp.where(eye, own, 0.0), j)
            theirs = link(nblocks * (1 - parity) + j)
            put(jnp.where(eye, theirs, 0.0), nblocks + 2 + j)
        other_slot = lower_at + (upper_at - lower_at) * parity
        put(has_other * tile_sum(other_slot), nblocks)
        put(tile_sum(upper_at + lower_at - other_slot), nblocks + 1)

    get_wself.wait()
    waiting = [get_wagg, get_wout]
    sig_grad = pre
    out_copy = None
    for layer in range(layers):
        own = ext[layer, pl.ds(0, rows), :]
        pre_self = dot(own, wself[layer], 1, 0)
        total = dot(adj[:, pl.ds(0, rows)], own, 1, 0)
        for copy in waiting:
            copy.wait()
        waiting = []
        for copy in halo:
            copy.wait()
        total += dot(
            adj[:, pl.ds(rows, rows + 2 * blk)], ext[layer, pl.ds(rows, rows + 2 * blk), :], 1, 0
        )
        agg_here = total.astype(BF16)
        agg[layer] = agg_here
        z = pre_self + dot(agg_here, wagg[layer], 1, 0)
        s = 1.0 / (1.0 + jnp.exp(-z))
        u = (z * s).astype(BF16)
        hidden[layer] = u
        y = dot(u, wout[layer], 1, 0)
        centred = y - jnp.mean(y, axis=-1, keepdims=True)
        inv = lax.rsqrt(jnp.mean(centred * centred, axis=-1, keepdims=True) + NORM_EPSILON)
        n = centred * inv
        new = (
            mask
            * (ext[layer, pl.ds(0, rows), :].astype(F32) + n * gain_vm[pl.ds(layer, 1), :])
        ).astype(BF16)
        if layer + 1 < layers:
            ext[layer + 1, pl.ds(0, rows), :] = new
            halo = start_halo(layer + 1)
        else:
            out_feats[...] = new
            out_copy = local(out_feats, out_feats_hbm)
        normed[layer] = n
        inv_std[layer] = inv
        sig_grad[layer] = s * (1.0 + z * (1.0 - s))

    half = slab // 2

    class Reducer:
        def __init__(self, layer, which, order):
            self.layer, self.which = layer, which
            self.plan = reduce_plan(half, order)
            self.off = which * half
            self.rows = half
            self.spots = []
            self.share = []
            at = 0
            for _, sent, halves in self.plan:
                self.spots.append(at)
                at += sent
            self.left = []

        def slot(self, ref, step):
            return ref.at[self.layer, self.which, pl.ds(self.spots[step], self.plan[step][1])]

        def at(self, off, size):
            return pl.ds(pl.multiple_of(off, ALIGN), size)

        def start(self, step):
            bit, size, halves = self.plan[step]
            away = self.off + (1 - bit_of(bit)) * size if halves else self.off
            src = self.slot(red_send, step)
            src[...] = grads[self.layer, self.at(away, size), :].astype(BF16)
            self.copy = remote(src, self.slot(red_recv, step), partner(bit))

        def finish(self, step):
            bit, size, halves = self.plan[step]
            self.copy.wait()
            came = self.slot(red_recv, step)[...].astype(F32)
            if halves:
                self.off = self.off + bit_of(bit) * size
                self.left.append((step, self.off, size))
                self.rows = size
                held = grads[self.layer, self.at(self.off, size), :]
            else:
                held = self.slot(red_send, step)[...].astype(F32)
            summed = held + came
            if step + 1 < len(self.plan):
                grads[self.layer, self.at(self.off, size), :] = summed
            else:
                full[self.layer, self.at(self.off, size), :] = summed.astype(BF16)

        def share_start(self):
            step, off, size = self.left.pop()
            region = full.at[self.layer, self.at(off, size)]
            self.copy = remote(region, region, partner(self.plan[step][0]))

        def share_finish(self):
            self.copy.wait()

    def flow(layer, gain_flow=None):
        parts = [Reducer(layer, 0, bits), Reducer(layer, 1, swapped)]
        steps = len(bits)
        for step in range(steps):
            for part in parts:
                part.start(step)
            if gain_flow is not None:
                gain_flow.start(step)
            yield
            for part in parts:
                part.finish(step)
            if gain_flow is not None:
                gain_flow.finish(step)
        while parts[0].left or parts[1].left:
            busy = [part for part in parts if part.left]
            for part in busy:
                part.share_start()
            yield
            for part in busy:
                part.share_finish()

    class Gains:
        def __init__(self, value):
            self.value = value

        def start(self, step):
            gain_send[step] = self.value
            self.copy = remote(gain_send.at[step], gain_recv.at[step], partner(bits[step]))

        def finish(self, step):
            self.copy.wait()
            self.value = self.value + gain_recv[step]

    flows = []

    def advance():
        for item in list(flows):
            try:
                next(item)
            except StopIteration:
                flows.remove(item)

    get_cotan.wait()
    grad = cotan[...].astype(F32)
    gain_rows = lax.broadcasted_iota(jnp.int32, gain_send.shape[1:], 0)
    gain_total = jnp.zeros(gain_send.shape[1:], F32)
    grad_copy = None
    for layer in reversed(range(layers)):
        n = normed[layer]
        masked = grad * mask
        scaled = masked * gain_vm[pl.ds(layer, 1), :]
        lifted = inv_std[layer] * (
            scaled
            - jnp.mean(scaled, axis=-1, keepdims=True)
            - n * jnp.mean(scaled * n, axis=-1, keepdims=True)
        )
        lifted = lifted.astype(BF16)
        back = dot(lifted, wout[layer], 1, 1)
        pre_grad = (back * sig_grad[layer]).astype(BF16)
        agg_back = dot(pre_grad, wagg[layer], 1, 1).astype(BF16)
        spread = dot(adj[:, pl.ds(rows, rows + 2 * blk)], agg_back, 0, 0)
        back_send[layer] = spread.astype(BF16)
        first = remote(
            back_send.at[layer, pl.ds(0, blk)], back_recv.at[layer, pl.ds(0, blk)], other
        )
        rest = pl.ds(blk, rows + blk)
        second = remote(back_send.at[layer, rest], back_recv.at[layer, rest], sibling)
        advance()
        gain_term = jnp.sum(masked * n, axis=0, keepdims=True)
        gain_total = jnp.where(gain_rows == layer, gain_term, gain_total)
        grads[layer, pl.ds(0, width), :] = dot(hidden[layer], lifted, 0, 0)
        grads[layer, pl.ds(width, width), :] = dot(ext[layer, pl.ds(0, rows), :], pre_grad, 0, 0)
        grads[layer, pl.ds(2 * width, width), :] = dot(agg[layer], pre_grad, 0, 0)
        gains = Gains(gain_total) if layer == 0 else None
        flows.append(flow(layer, gains))
        advance()
        grad = masked + dot(pre_grad, wself[layer], 1, 1)
        grad += dot(adj[:, pl.ds(0, rows)], agg_back, 0, 0)
        first.wait()
        second.wait()
        from_other = back_recv[layer, pl.ds(0, blk), :].astype(F32)
        from_sibling = back_recv[layer, pl.ds(blk, blk), :].astype(F32)
        pieces = [
            hot(to_other, j) * from_other + hot(to_sibling, j) * from_sibling
            for j in range(nblocks)
        ]
        grad += back_recv[layer, pl.ds(2 * blk, rows), :].astype(F32)
        grad += jnp.concatenate(pieces, axis=0)
        if layer > 0:
            advance()
    feats_grad[...] = (grad * mask).astype(BF16)
    grad_copy = local(feats_grad, feats_grad_hbm)
    while flows:
        advance()
    gain_grad_vm[...] = gains.value[0:layers]

    last = []
    for layer in range(layers):
        for part, target in enumerate((out_grad_hbm, self_grad_hbm, agg_grad_hbm)):
            last.append(local(full.at[layer, pl.ds(part * width, width)], target.at[layer]))
    for copy in last:
        copy.wait()
    out_copy.wait()
    grad_copy.wait()
    assert sems.used <= sem_count, sems.used


def per_device(
    count,
    node_feats,
    cotangent,
    tile_val,
    tile_src,
    halo_list,
    block_count,
    coarse_src,
    coarse_val,
    w_self,
    w_agg,
    w_out,
    norm_gain,
):
    rows, width = node_feats.shape
    nblocks, ktiles, blk, _ = tile_val.shape
    layers = w_self.shape[0]
    bits, _ = dim_orders(count)
    stages = len(bits)
    reduce_rows = sum(size for _, size, _ in reduce_plan(3 * width // 2, bits))
    sem_count = 32 + 10 * layers + 8 * layers * stages + 2 * stages + 4 * layers
    ext_rows = 2 * rows + 2 * blk
    any_space = pl.BlockSpec(memory_space=pl.ANY)
    smem = pl.BlockSpec(memory_space=pltpu.SMEM)
    vmem = pl.BlockSpec(memory_space=pltpu.VMEM)
    shape = jax.ShapeDtypeStruct
    weights = (layers, width, width)
    outs = pl.pallas_call(
        functools.partial(kernel, count, sem_count),
        out_shape=(
            shape((rows, width), BF16),
            shape((rows, width), BF16),
            shape(weights, BF16),
            shape(weights, BF16),
            shape(weights, BF16),
            shape((layers, width), F32),
        ),
        in_specs=[smem] * 5 + [any_space] * 6 + [vmem],
        out_specs=(any_space,) * 5 + (vmem,),
        scratch_shapes=[
            pltpu.VMEM((rows, width), BF16),
            pltpu.VMEM((rows, width), BF16),
            pltpu.VMEM(tile_val.shape, BF16),
            pltpu.VMEM(weights, BF16),
            pltpu.VMEM(weights, BF16),
            pltpu.VMEM(weights, BF16),
            pltpu.VMEM((rows, ext_rows), BF16),
            pltpu.VMEM((layers, ext_rows, width), BF16),
            pltpu.VMEM((layers, 2 * blk, width), BF16),
            pltpu.VMEM((layers, rows, width), BF16),
            pltpu.VMEM((layers, rows, width), F32),
            pltpu.VMEM((layers, rows, width), BF16),
            pltpu.VMEM((layers, rows, width), F32),
            pltpu.VMEM((layers, rows, 1), F32),
            pltpu.VMEM((rows, width), BF16),
            pltpu.VMEM((rows, width), BF16),
            pltpu.VMEM((layers, rows + 2 * blk, width), BF16),
            pltpu.VMEM((layers, rows + 2 * blk, width), BF16),
            pltpu.VMEM((layers, 3 * width, width), F32),
            pltpu.VMEM((layers, 2, reduce_rows, width), BF16),
            pltpu.VMEM((layers, 2, reduce_rows, width), BF16),
            pltpu.VMEM((layers, 3 * width, width), BF16),
            pltpu.VMEM((stages, 8, width), F32),
            pltpu.VMEM((stages, 8, width), F32),
            pltpu.SemaphoreType.DMA((sem_count,)),
        ],
        compiler_params=pltpu.CompilerParams(
            collective_id=0, has_side_effects=True, vmem_limit_bytes=50 * 2**20
        ),
        cost_estimate=pl.CostEstimate(
            flops=3 * 10**9, bytes_accessed=10 * 2**20, transcendentals=2 * layers * rows * width
        ),
    )(
        tile_src,
        halo_list,
        block_count,
        coarse_src,
        coarse_val,
        node_feats,
        cotangent,
        tile_val,
        w_self,
        w_agg,
        w_out,
        norm_gain,
    )
    return tuple(outs)


def solution(mesh):
    nodes = P(("groups", "gx"), None)
    return jax.shard_map(
        functools.partial(per_device, mesh.shape["gx"]),
        mesh=mesh,
        in_specs=(
            nodes,
            nodes,
            P(("groups", "gx"), None, None, None),
            nodes,
            P(("groups", "gx"), None, None),
            P(("groups", "gx")),
            nodes,
            nodes,
            P(),
            P(),
            P(),
            P(),
        ),
        out_specs=(
            nodes,
            nodes,
            P("groups", None, None),
            P("groups", None, None),
            P("groups", None, None),
            P("groups", None),
        ),
        check_vma=False,
    )
```

profile of v0, /device:TPU:0, one launch (start us, length us, event | category | flops | bytes accessed | tf_op | source)
XLA Modules:
  0.0 89.4 jit_solution(6347912032100823432)
XLA Ops:
  0.6 0.0 copy-start.8
  0.6 0.0 copy-start.5
  0.7 0.0 copy-start.6
  1.3 0.0 copy-done.8
  1.3 0.0 copy-start.4
  1.4 0.1 copy.18.halo_list
  1.4 0.0 copy-done.5
  1.4 0.0 copy-done.6
  1.5 0.6 copy-done.4
  2.0 0.0 copy-start
  2.0 0.9 %copy-done = bf16[256,512]{1,0:T(8,128)(2,1)S(1)} copy-done((bf16[256,512]{1,0:T(8,128)(2,1)S(1)}, bf16[256,512]{1,0:T(8,128)(2,1)}, u32[]{:S(2)}) %copy-start) | copy-done | bytes 262168
  3.0 0.0 copy-start.1
  3.0 0.9 %copy-done.1 = bf16[256,512]{1,0:T(8,128)(2,1)S(1)} copy-done((bf16[256,512]{1,0:T(8,128)(2,1)S(1)}, bf16[256,512]{1,0:T(8,128)(2,1)}, u32[]{:S(2)}) %copy-start.1) | copy-done | bytes 262168
  3.9 0.0 copy-start.2
  3.9 0.9 %copy-done.2 = bf16[2,4,128,128]{3,2,1,0:T(8,128)(2,1)S(1)} copy-done((bf16[2,4,128,128]{3,2,1,0:T(8,128)(2,1)S(1)}, bf16[2,4,128,128]{3,2,1,0:T(8,128)(2,1)}, u32[]{:S(2)}) %copy-start.2) | copy-done | bytes 262168
  4.9 0.0 copy-start.3
  4.9 0.7 copy-done.3
  5.6 78.3 %shard_map.163 = (bf16[256,512]{1,0:T(8,128)(2,1)S(1)}, bf16[256,512]{1,0:T(8,128)(2,1)S(1)}, bf16[2,512,512]{2,1,0:T(8,128)(2,1)S(1)}, bf16[2,512,512]{2,1,0:T(...) custom-call(s32[2,4]{1,0:T(2,128)S(1)} %copy-done.4, s32[1,2,1]{2,1,0:T(2,128)S(1)} %copy.18.halo_list, ...), custom_call_target="tpu_custom_call" | custom-call | flops 3000000000 | bytes 10485760 | tf_op jit(solution)/shard_map/pallas_call | solution.py:446
  83.9 0.7 copy.26
  84.6 0.7 copy.27
  85.3 1.0 %copy.28 = bf16[2,512,512]{2,1,0:T(8,128)(2,1)} copy(bf16[2,512,512]{2,1,0:T(8,128)(2,1)S(1)} %get-tuple-element.14) | data formatting | bytes 2097152
  86.3 0.0 copy-start.7
  86.3 1.0 %copy.29 = bf16[2,512,512]{2,1,0:T(8,128)(2,1)} copy(bf16[2,512,512]{2,1,0:T(8,128)(2,1)S(1)} %get-tuple-element.15) | data formatting | bytes 2097152
  87.2 0.6 copy-done.7
  87.9 1.0 %copy.30 = bf16[2,512,512]{2,1,0:T(8,128)(2,1)} copy(bf16[2,512,512]{2,1,0:T(8,128)(2,1)S(1)} %copy-done.7) | data formatting | bytes 2097152
  88.8 0.6 copy.31
Async XLA Ops:
  0.6 0.7 copy-start.8
  0.6 0.8 copy-start.5
  0.7 0.8 copy-start.6
  1.3 0.7 copy-start.4
  2.0 0.9 %copy-start = (bf16[256,512]{1,0:T(8,128)(2,1)S(1)}, bf16[256,512]{1,0:T(8,128)(2,1)}, u32[]{:S(2)}) copy-start(bf16[256,512]{1,0:T(8,128)(2,1)} %feats_hbm.1) | copy-start | bytes 786436
  3.0 0.9 %copy-start.1 = (bf16[256,512]{1,0:T(8,128)(2,1)S(1)}, bf16[256,512]{1,0:T(8,128)(2,1)}, u32[]{:S(2)}) copy-start(bf16[256,512]{1,0:T(8,128)(2,1)} %cotan_hbm.1) | copy-start | bytes 786436
  3.9 0.9 %copy-start.2 = (bf16[2,4,128,128]{3,2,1,0:T(8,128)(2,1)S(1)}, bf16[2,4,128,128]{3,2,1,0:T(8,128)(2,1)}, u32[]{:S(2)}) copy-start(bf16[2,4,128,128]{3,2,1,0:T(8,128)(2,1)} %tiles_hbm.1) | copy-start | bytes 786436
  4.9 0.7 copy-start.3
  86.3 1.6 %copy-start.7 = (bf16[2,512,512]{2,1,0:T(8,128)(2,1)S(1)}, bf16[2,512,512]{2,1,0:T(8,128)(2,1)}, u32[]{:S(2)}) copy-start(bf16[2,512,512]{2,1,0:T(8,128)(2,1)} %get-tuple-element.16) | copy-start | bytes 3145732
where the time goes:
time: 89.8 us; the launch traced here: 89.4 us
  Pallas kernels  78.3 us (87%)
  local copies, waits for them, and re-layouts  9.75 us (11%)
  between operations  1.36 us (2%)
    pallas_call x1, Pallas kernels, per_device(): pl.pallas_call(functools.partial(kernel, count, sem_count), out_shape=(sh...  78.3 us
    unnamed x25, local copies, waits for them, and re-layouts  9.75 us

commit v1 on v0

--- a/solution.py
+++ b/solution.py
@@ -20,24 +20,33 @@
     )
 
 
-def reduce_plan(rows, bits):
+def reduce_plan(rows, groups):
     plan = []
-    for bit in bits:
-        halves = rows % (2 * ALIGN) == 0
-        if halves:
-            rows //= 2
-        plan.append((bit, rows, halves))
+    for bit, size in groups:
+        split = rows % (size * ALIGN) == 0
+        if split:
+            rows //= size
+        plan.append((bit, size, rows, split))
     return plan
 
 
-def dim_orders(count):
-    bits = []
-    while 2 ** (len(bits) + 1) <= count:
-        bits.append(len(bits))
-    swapped = list(bits)
-    if len(bits) >= 3:
+def slot_rows(plan):
+    return sum((size - 1) * rows for _, size, rows, _ in plan)
+
+
+def group_orders(count):
+    groups, bit = [], 0
+    while 2**bit < count:
+        groups.append((bit, 2))
+        bit += 1
+    swapped = list(groups)
+    if len(groups) >= 3:
         swapped[1], swapped[2] = swapped[2], swapped[1]
-    return bits, swapped
+    return groups, swapped, groups
+
+
+def part_rows(width):
+    return (width, width, width)
 
 
 class Sems:
@@ -108,20 +117,38 @@
     across = me - 1 + 2 * parity
     other = (across + count) % count
     has_other = jnp.where(across == other, 1.0, 0.0).astype(F32)
-    bits, swapped = dim_orders(count)
-
-    def bit_of(bit):
-        return (me // 2**bit) % 2
-
-    def partner(bit):
-        return me + (1 - 2 * bit_of(bit)) * 2**bit
+    orders = group_orders(count)
+
+    def place(bit, size):
+        return (me // 2**bit) % size
+
+    def peer(bit, size, by):
+        mine = place(bit, size)
+        return me + ((mine + by) % size - mine) * 2**bit
 
     def local(src, dst):
         copy = pltpu.make_async_copy(src, dst, sems.take())
         copy.start()
         return copy
 
-    def remote(src, dst, to):
+    class AcrossCopy:
+        def __init__(self, src, dst):
+            self.copy = remote(src, dst, other, start=False)
+
+            @pl.when(across == other)
+            def _():
+                self.copy.start()
+
+            @pl.when(across != other)
+            def _():
+                dst[...] = jnp.zeros(dst.shape, dst.dtype)
+
+        def wait(self):
+            @pl.when(across == other)
+            def _():
+                self.copy.wait()
+
+    def remote(src, dst, to, start=True):
         copy = pltpu.make_async_remote_copy(
             src_ref=src,
             dst_ref=dst,
@@ -130,7 +157,8 @@
             device_id={"gx": to},
             device_id_type=MESH,
         )
-        copy.start()
+        if start:
+            copy.start()
         return copy
 
     get_feats = local(feats_hbm, feats)
@@ -141,9 +169,9 @@
     get_cotan = local(cotan_hbm, cotan)
 
     barrier = pltpu.get_barrier_semaphore()
-    peers = [partner(bit) for bit in bits] + [other]
-    for peer in peers:
-        pl.semaphore_signal(barrier, inc=1, device_id={"gx": peer}, device_id_type=MESH)
+    peers = [peer(bit, size, by) for bit, size in orders[0] for by in range(1, size)] + [other]
+    for to in peers:
+        pl.semaphore_signal(barrier, inc=1, device_id={"gx": to}, device_id_type=MESH)
 
     row_ids = lax.broadcasted_iota(jnp.int32, (rows, 1), 0)
     mask = jnp.where(row_ids < block_count[0] * blk, 1.0, 0.0).astype(F32)
@@ -163,8 +191,8 @@
     def start_halo(layer):
         here = ext.at[layer]
         halo_send[layer, pl.ds(0, blk), :] = pick(here, to_other)
-        first = remote(
-            halo_send.at[layer, pl.ds(0, blk)], ext.at[layer, pl.ds(rows, blk)], other
+        first = AcrossCopy(
+            halo_send.at[layer, pl.ds(0, blk)], ext.at[layer, pl.ds(rows, blk)]
         )
         halo_send[layer, pl.ds(blk, blk), :] = pick(here, to_sibling)
         second = remote(
@@ -254,92 +282,94 @@
         inv_std[layer] = inv
         sig_grad[layer] = s * (1.0 + z * (1.0 - s))
 
-    half = slab // 2
-
     class Reducer:
-        def __init__(self, layer, which, order):
-            self.layer, self.which = layer, which
-            self.plan = reduce_plan(half, order)
-            self.off = which * half
-            self.rows = half
-            self.spots = []
-            self.share = []
-            at = 0
-            for _, sent, halves in self.plan:
-                self.spots.append(at)
-                at += sent
+        def __init__(self, layer, which, gains=None):
+            self.layer, self.which, self.gains = layer, which, gains
+            parts = part_rows(width)
+            self.plan = reduce_plan(parts[which], orders[which])
+            self.off = sum(parts[:which])
+            self.base = sum(slot_rows(reduce_plan(parts[i], orders[i])) for i in range(which))
             self.left = []
 
-        def slot(self, ref, step):
-            return ref.at[self.layer, self.which, pl.ds(self.spots[step], self.plan[step][1])]
+        def slot(self, ref, step, by):
+            at = self.base + slot_rows(self.plan[:step]) + (by - 1) * self.plan[step][2]
+            return ref.at[self.layer, pl.ds(at, self.plan[step][2])]
 
         def at(self, off, size):
             return pl.ds(pl.multiple_of(off, ALIGN), size)
 
         def start(self, step):
-            bit, size, halves = self.plan[step]
-            away = self.off + (1 - bit_of(bit)) * size if halves else self.off
-            src = self.slot(red_send, step)
-            src[...] = grads[self.layer, self.at(away, size), :].astype(BF16)
-            self.copy = remote(src, self.slot(red_recv, step), partner(bit))
+            bit, size, share, split = self.plan[step]
+            mine = place(bit, size)
+            self.copies = []
+            for by in range(1, size):
+                away = self.off + (mine + by) % size * share if split else self.off
+                src = self.slot(red_send, step, by)
+                src[...] = grads[self.layer, self.at(away, share), :].astype(BF16)
+                self.copies.append(remote(src, self.slot(red_recv, step, by), peer(bit, size, by)))
+            if self.gains is not None:
+                self.gains.start(step)
 
         def finish(self, step):
-            bit, size, halves = self.plan[step]
-            self.copy.wait()
-            came = self.slot(red_recv, step)[...].astype(F32)
-            if halves:
-                self.off = self.off + bit_of(bit) * size
-                self.left.append((step, self.off, size))
-                self.rows = size
-                held = grads[self.layer, self.at(self.off, size), :]
+            bit, size, share, split = self.plan[step]
+            if split:
+                self.off = self.off + place(bit, size) * share
+                self.left.append((bit, size, self.off, share))
+                summed = grads[self.layer, self.at(self.off, share), :]
             else:
-                held = self.slot(red_send, step)[...].astype(F32)
-            summed = held + came
+                summed = self.slot(red_send, step, 1)[...].astype(F32)
+            for copy in self.copies:
+                copy.wait()
+            for by in range(1, size):
+                summed = summed + self.slot(red_recv, step, by)[...].astype(F32)
             if step + 1 < len(self.plan):
-                grads[self.layer, self.at(self.off, size), :] = summed
+                grads[self.layer, self.at(self.off, share), :] = summed
             else:
-                full[self.layer, self.at(self.off, size), :] = summed.astype(BF16)
-
-        def share_start(self):
-            step, off, size = self.left.pop()
-            region = full.at[self.layer, self.at(off, size)]
-            self.copy = remote(region, region, partner(self.plan[step][0]))
-
-        def share_finish(self):
-            self.copy.wait()
-
-    def flow(layer, gain_flow=None):
-        parts = [Reducer(layer, 0, bits), Reducer(layer, 1, swapped)]
-        steps = len(bits)
-        for step in range(steps):
-            for part in parts:
-                part.start(step)
-            if gain_flow is not None:
-                gain_flow.start(step)
-            yield
-            for part in parts:
-                part.finish(step)
-            if gain_flow is not None:
-                gain_flow.finish(step)
-        while parts[0].left or parts[1].left:
-            busy = [part for part in parts if part.left]
-            for part in busy:
-                part.share_start()
-            yield
-            for part in busy:
-                part.share_finish()
+                full[self.layer, self.at(self.off, share), :] = summed.astype(BF16)
+            if self.gains is not None:
+                self.gains.finish(step)
+
+        def flow(self):
+            for step in range(len(self.plan)):
+                self.start(step)
+                yield
+                self.finish(step)
+            for bit, size, off, share in reversed(self.left):
+                region = full.at[self.layer, self.at(off, share)]
+                copies = [remote(region, region, peer(bit, size, by)) for by in range(1, size)]
+                yield
+                for copy in copies:
+                    copy.wait()
 
     class Gains:
         def __init__(self, value):
-            self.value = value
+            self.value, self.used = value, 0
 
         def start(self, step):
+            bit, size = orders[0][step]
+            self.copies = []
+            self.slots = range(self.used, self.used + size - 1)
+            self.used += size - 1
             gain_send[step] = self.value
-            self.copy = remote(gain_send.at[step], gain_recv.at[step], partner(bits[step]))
+            for by, slot in enumerate(self.slots, 1):
+                self.copies.append(
+                    remote(gain_send.at[step], gain_recv.at[slot], peer(bit, size, by))
+                )
 
         def finish(self, step):
-            self.copy.wait()
-            self.value = self.value + gain_recv[step]
+            bit, size = orders[0][step]
+            for copy in self.copies:
+                copy.wait()
+            if size == 2:
+                self.value = self.value + gain_recv[self.slots[0]]
+                return
+            mine = place(bit, size)
+            terms = [self.value] + [gain_recv[slot] for slot in self.slots]
+            total = jnp.zeros_like(self.value)
+            for want in range(size):
+                for by in range(size):
+                    total = total + jnp.where((mine - by + size) % size == want, 1.0, 0.0) * terms[by]
+            self.value = total
 
     flows = []
 
@@ -349,6 +379,14 @@
                 next(item)
             except StopIteration:
                 flows.remove(item)
+
+    gains = None
+
+    def begin(layer, which, left, right):
+        grads[layer, pl.ds(which * width, width), :] = dot(left, right, 0, 0)
+        last = gains if layer == 0 and which == 2 else None
+        flows.append(Reducer(layer, which, last).flow())
+        next(flows[-1])
 
     get_cotan.wait()
     grad = cotan[...].astype(F32)
@@ -365,27 +403,31 @@
             - n * jnp.mean(scaled * n, axis=-1, keepdims=True)
         )
         lifted = lifted.astype(BF16)
+        if layer == 0:
+            begin(layer, 0, hidden[layer], lifted)
         back = dot(lifted, wout[layer], 1, 1)
         pre_grad = (back * sig_grad[layer]).astype(BF16)
+        gain_term = jnp.sum(masked * n, axis=0, keepdims=True)
+        gain_total = jnp.where(gain_rows == layer, gain_term, gain_total)
+        if layer == 0:
+            gains = Gains(gain_total)
+            begin(layer, 1, ext[layer, pl.ds(0, rows), :], pre_grad)
+            begin(layer, 2, agg[layer], pre_grad)
         agg_back = dot(pre_grad, wagg[layer], 1, 1).astype(BF16)
         spread = dot(adj[:, pl.ds(rows, rows + 2 * blk)], agg_back, 0, 0)
         back_send[layer] = spread.astype(BF16)
-        first = remote(
-            back_send.at[layer, pl.ds(0, blk)], back_recv.at[layer, pl.ds(0, blk)], other
+        first = AcrossCopy(
+            back_send.at[layer, pl.ds(0, blk)], back_recv.at[layer, pl.ds(0, blk)]
         )
         rest = pl.ds(blk, rows + blk)
         second = remote(back_send.at[layer, rest], back_recv.at[layer, rest], sibling)
-        advance()
-        gain_term = jnp.sum(masked * n, axis=0, keepdims=True)
-        gain_total = jnp.where(gain_rows == layer, gain_term, gain_total)
-        grads[layer, pl.ds(0, width), :] = dot(hidden[layer], lifted, 0, 0)
-        grads[layer, pl.ds(width, width), :] = dot(ext[layer, pl.ds(0, rows), :], pre_grad, 0, 0)
-        grads[layer, pl.ds(2 * width, width), :] = dot(agg[layer], pre_grad, 0, 0)
-        gains = Gains(gain_total) if layer == 0 else None
-        flows.append(flow(layer, gains))
-        advance()
+        if layer > 0:
+            begin(layer, 0, hidden[layer], lifted)
+            begin(layer, 1, ext[layer, pl.ds(0, rows), :], pre_grad)
+            begin(layer, 2, agg[layer], pre_grad)
         grad = masked + dot(pre_grad, wself[layer], 1, 1)
         grad += dot(adj[:, pl.ds(0, rows)], agg_back, 0, 0)
+        advance()
         first.wait()
         second.wait()
         from_other = back_recv[layer, pl.ds(0, blk), :].astype(F32)
@@ -396,8 +438,6 @@
         ]
         grad += back_recv[layer, pl.ds(2 * blk, rows), :].astype(F32)
         grad += jnp.concatenate(pieces, axis=0)
-        if layer > 0:
-            advance()
     feats_grad[...] = (grad * mask).astype(BF16)
     grad_copy = local(feats_grad, feats_grad_hbm)
     while flows:
@@ -413,6 +453,32 @@
     out_copy.wait()
     grad_copy.wait()
     assert sems.used <= sem_count, sems.used
+
+
+def copy_kernel(*refs):
+    count = len(refs) // 3
+    sources, targets, stages, sem = refs[:count], refs[count : 2 * count], refs[2 * count : -1], refs[-1]
+    loads, stores = [], []
+    for i in range(count):
+        loads.append(pltpu.make_async_copy(sources[i], stages[i], sem.at[0, i]))
+        loads[-1].start()
+    for i in range(count):
+        loads[i].wait()
+        stores.append(pltpu.make_async_copy(stages[i], targets[i], sem.at[1, i]))
+        stores[-1].start()
+    for store in stores:
+        store.wait()
+
+
+def copied_out(arrays):
+    return pl.pallas_call(
+        copy_kernel,
+        out_shape=tuple(jax.ShapeDtypeStruct(x.shape, x.dtype) for x in arrays),
+        in_specs=[pl.BlockSpec(memory_space=pl.ANY)] * len(arrays),
+        out_specs=(pl.BlockSpec(memory_space=pl.ANY),) * len(arrays),
+        scratch_shapes=[pltpu.VMEM(x.shape, x.dtype) for x in arrays]
+        + [pltpu.SemaphoreType.DMA((2, len(arrays)))],
+    )(*arrays)
 
 
 def per_device(
@@ -433,10 +499,12 @@
     rows, width = node_feats.shape
     nblocks, ktiles, blk, _ = tile_val.shape
     layers = w_self.shape[0]
-    bits, _ = dim_orders(count)
-    stages = len(bits)
-    reduce_rows = sum(size for _, size, _ in reduce_plan(3 * width // 2, bits))
-    sem_count = 32 + 10 * layers + 8 * layers * stages + 2 * stages + 4 * layers
+    orders = group_orders(count)
+    stages = len(orders[0])
+    links = sum(size - 1 for _, size in orders[0])
+    plans = [reduce_plan(rows, order) for rows, order in zip(part_rows(width), orders)]
+    reduce_rows = sum(slot_rows(plan) for plan in plans)
+    sem_count = 32 + 14 * layers + 4 * len(plans) * layers * links + 2 * links
     ext_rows = 2 * rows + 2 * blk
     any_space = pl.BlockSpec(memory_space=pl.ANY)
     smem = pl.BlockSpec(memory_space=pltpu.SMEM)
@@ -475,15 +543,15 @@
             pltpu.VMEM((layers, rows + 2 * blk, width), BF16),
             pltpu.VMEM((layers, rows + 2 * blk, width), BF16),
             pltpu.VMEM((layers, 3 * width, width), F32),
-            pltpu.VMEM((layers, 2, reduce_rows, width), BF16),
-            pltpu.VMEM((layers, 2, reduce_rows, width), BF16),
+            pltpu.VMEM((layers, reduce_rows, width), BF16),
+            pltpu.VMEM((layers, reduce_rows, width), BF16),
             pltpu.VMEM((layers, 3 * width, width), BF16),
             pltpu.VMEM((stages, 8, width), F32),
-            pltpu.VMEM((stages, 8, width), F32),
+            pltpu.VMEM((links, 8, width), F32),
             pltpu.SemaphoreType.DMA((sem_count,)),
         ],
         compiler_params=pltpu.CompilerParams(
-            collective_id=0, has_side_effects=True, vmem_limit_bytes=50 * 2**20
+            collective_id=0, has_side_effects=True, vmem_limit_bytes=63 * 2**20
         ),
         cost_estimate=pl.CostEstimate(
             flops=3 * 10**9, bytes_accessed=10 * 2**20, transcendentals=2 * layers * rows * width
@@ -502,7 +570,7 @@
         w_out,
         norm_gain,
     )
-    return tuple(outs)
+    return copied_out(outs)
 
 
 def solution(mesh):

time: 89.8 us -> 74.5 us (0.83)
  local copies, waits for them, and re-layouts: 9.75 us -> 0.65 us
  Pallas kernels: 78.3 us -> 72.4 us
    pallas_call x1, Pallas kernels: 78.3 us -> 69.1 us  [per_device(): pl.pallas_call(functools.partial(kernel, count, sem_count), out_shape=(sh...]
    unnamed x25 -> x3, local copies, waits for them, and re-layouts: 9.75 us -> 0.65 us
    pallas_call x0 -> x1, Pallas kernels: none -> 3.29 us  [copied_out(): pl.pallas_call(copy_kernel, out_shape=tuple((jax.ShapeDtypeStruct(x.shape...]
where the time goes in v1:
time: 74.5 us; the launch traced here: 74.4 us
  Pallas kernels  72.4 us (97%)
  between operations  1.32 us (2%)
    pallas_call x1, Pallas kernels, per_device(): pl.pallas_call(functools.partial(kernel, count, sem_count), out_shape=(sh...  69.1 us
    pallas_call x1, Pallas kernels, copied_out(): pl.pallas_call(copy_kernel, out_shape=tuple((jax.ShapeDtypeStruct(x.shape...  3.29 us

profile of v1, /device:TPU:0, one launch (start us, length us, event | category | flops | bytes accessed | tf_op | source)
XLA Modules:
  0.0 74.4 jit_solution(16192253767382674579)
XLA Ops:
  0.6 0.0 copy-start
  1.3 0.0 copy-done
  1.3 0.6 copy.18.halo_list
  2.0 69.1 %shard_map.163 = (bf16[256,512]{1,0:T(8,128)(2,1)}, bf16[256,512]{1,0:T(8,128)(2,1)}, bf16[2,512,512]{2,1,0:T(8,128)(2,1)}, bf16[2,512,512]{2,1,0:T(8,128)(2,1)}...) custom-call(s32[2,4]{1,0:T(2,128)} %tile_src.1, s32[1,2,1]{2,1,0:T(2,128)} %copy.18.halo_list, s32[1]{0:T(128)S(6)} %copy.19.block_count, ...), custom_call_target="tpu_custom_call" | custom-call | flops 3000000000 | bytes 10485760 | tf_op jit(solution)/shard_map/pallas_call | solution.py:514
  71.1 3.3 %shard_map.164 = (bf16[256,512]{1,0:T(8,128)(2,1)}, bf16[256,512]{1,0:T(8,128)(2,1)}, bf16[2,512,512]{2,1,0:T(8,128)(2,1)}, bf16[2,512,512]{2,1,0:T(8,128)(2,1)}...) custom-call(bf16[256,512]{1,0:T(8,128)(2,1)} %get-tuple-element.12.refs_0_, bf16[256,512]{1,0:T(8,128)(2,1)} %get-tuple-element.13.refs_1_, ...), custom_call_target="tpu_custom_call" | custom-call | tf_op jit(solution)/shard_map/pallas_call | solution.py:474
Async XLA Ops:
  0.6 0.7 copy-start

commit v2 on v1

--- a/solution.py
+++ b/solution.py
@@ -340,6 +340,9 @@
                 yield
                 for copy in copies:
                     copy.wait()
+            done = full.at[self.layer, pl.ds(self.which * width, width)]
+            targets = (out_grad_hbm, self_grad_hbm, agg_grad_hbm)
+            last.append(local(done, targets[self.which].at[self.layer]))
 
     class Gains:
         def __init__(self, value):
@@ -381,6 +384,7 @@
                 flows.remove(item)
 
     gains = None
+    last = []
 
     def begin(layer, which, left, right):
         grads[layer, pl.ds(which * width, width), :] = dot(left, right, 0, 0)
@@ -444,10 +448,6 @@
         advance()
     gain_grad_vm[...] = gains.value[0:layers]
 
-    last = []
-    for layer in range(layers):
-        for part, target in enumerate((out_grad_hbm, self_grad_hbm, agg_grad_hbm)):
-            last.append(local(full.at[layer, pl.ds(part * width, width)], target.at[layer]))
     for copy in last:
         copy.wait()
     out_copy.wait()
@@ -458,13 +458,19 @@
 def copy_kernel(*refs):
     count = len(refs) // 3
     sources, targets, stages, sem = refs[:count], refs[count : 2 * count], refs[2 * count : -1], refs[-1]
+    chunks = []
+    for refs_here in zip(sources, stages, targets):
+        if len(refs_here[0].shape) == 3:
+            chunks += [tuple(ref.at[i] for ref in refs_here) for i in range(refs_here[0].shape[0])]
+        else:
+            chunks.append(refs_here)
     loads, stores = [], []
-    for i in range(count):
-        loads.append(pltpu.make_async_copy(sources[i], stages[i], sem.at[0, i]))
+    for i, (source, stage, _) in enumerate(chunks):
+        loads.append(pltpu.make_async_copy(source, stage, sem.at[0, i]))
         loads[-1].start()
-    for i in range(count):
+    for i, (_, stage, target) in enumerate(chunks):
         loads[i].wait()
-        stores.append(pltpu.make_async_copy(stages[i], targets[i], sem.at[1, i]))
+        stores.append(pltpu.make_async_copy(stage, target, sem.at[1, i]))
         stores[-1].start()
     for store in stores:
         store.wait()
@@ -477,7 +483,7 @@
         in_specs=[pl.BlockSpec(memory_space=pl.ANY)] * len(arrays),
         out_specs=(pl.BlockSpec(memory_space=pl.ANY),) * len(arrays),
         scratch_shapes=[pltpu.VMEM(x.shape, x.dtype) for x in arrays]
-        + [pltpu.SemaphoreType.DMA((2, len(arrays)))],
+        + [pltpu.SemaphoreType.DMA((2, sum(x.shape[0] if x.ndim == 3 else 1 for x in arrays)))],
     )(*arrays)
 
 

time: 74.5 us -> 73.7 us (0.989)
  Pallas kernels: 72.4 us -> 71.5 us
    pallas_call x1, Pallas kernels: 69.1 us -> 68.3 us  [per_device(): pl.pallas_call(functools.partial(kernel, count, sem_count), out_shape=(sh...]
where the time goes in v2:
time: 73.7 us; the launch traced here: 73.5 us
  Pallas kernels  71.5 us (97%)
  between operations  1.32 us (2%)
    pallas_call x1, Pallas kernels, per_device(): pl.pallas_call(functools.partial(kernel, count, sem_count), out_shape=(sh...  68.3 us
    pallas_call x1, Pallas kernels, copied_out(): pl.pallas_call(copy_kernel, out_shape=tuple((jax.ShapeDtypeStruct(x.shape...  3.28 us

profile of v2, /device:TPU:0, one launch (start us, length us, event | category | flops | bytes accessed | tf_op | source)
XLA Modules:
  0.0 73.5 jit_solution(13418669070541904700)
XLA Ops:
  0.6 0.0 copy-start
  1.3 0.0 copy-done
  1.3 0.6 copy.18.halo_list
  2.0 68.3 %shard_map.163 = (bf16[256,512]{1,0:T(8,128)(2,1)}, bf16[256,512]{1,0:T(8,128)(2,1)}, bf16[2,512,512]{2,1,0:T(8,128)(2,1)}, bf16[2,512,512]{2,1,0:T(8,128)(2,1)}...) custom-call(s32[2,4]{1,0:T(2,128)} %tile_src.1, s32[1,2,1]{2,1,0:T(2,128)} %copy.18.halo_list, s32[1]{0:T(128)S(6)} %copy.19.block_count, ...), custom_call_target="tpu_custom_call" | custom-call | flops 3000000000 | bytes 10485760 | tf_op jit(solution)/shard_map/pallas_call | solution.py:520
  70.2 3.3 %shard_map.164 = (bf16[256,512]{1,0:T(8,128)(2,1)}, bf16[256,512]{1,0:T(8,128)(2,1)}, bf16[2,512,512]{2,1,0:T(8,128)(2,1)}, bf16[2,512,512]{2,1,0:T(8,128)(2,1)}...) custom-call(bf16[256,512]{1,0:T(8,128)(2,1)} %get-tuple-element.12.refs_0_, bf16[256,512]{1,0:T(8,128)(2,1)} %get-tuple-element.13.refs_1_, ...), custom_call_target="tpu_custom_call" | custom-call | tf_op jit(solution)/shard_map/pallas_call | solution.py:480
Async XLA Ops:
  0.6 0.7 copy-start
